TPU v7x, 256 devices: a whole 4x4x8 slice. The times are simulated.
256 devices in a mesh: tm: 4 (over y), height: 4 (over x), width: 16 (over z, core).
Axes of the slice: x: 4, y: 4, z: 8, core: 2. Of those that a mesh axis runs over, the one named last changes fastest.
Arguments:
- features: bfloat16 [16, 32, 160, 384], P('tm', 'height', 'width'), may hold values from -6 to 6
- first_gain: float32 [384], replicated, may hold values from 0.5 to 2
- first_kernel: bfloat16 [27, 384, 384], P(None, ('height', 'width')), may hold values from -0.0625 to 0.0625
- first_bias: float32 [384], replicated, may hold values from -3 to 3
- second_gain: float32 [384], replicated, may hold values from 0.5 to 2
- second_kernel: bfloat16 [27, 384, 384], P(None, ('height', 'width')), may hold values from -0.0625 to 0.0625
- second_bias: float32 [384], replicated, may hold values from -3 to 3
Outputs:
- block_out: bfloat16 [16, 32, 160, 384], P('tm', 'height', 'width')
All inputs are finite; a program needn't handle non-finite values.
Results may differ from a plain program's by a relative error of at most 0.012.
Values may be sent and summed in bfloat16 or wider, within the bound.
No kernel may reach another device: no remote copies, remote signals or barrier semaphores. Data moves between devices by JAX's collectives and lax.ppermute only.
A program may use at most 128 MiB of HBM per device.

v0:
```python
import jax
import jax.numpy as jnp
from jax import lax
from jax.sharding import PartitionSpec as P


def passed_along(x, axis, by):
    devices = lax.axis_size(axis)
    pairs = [(i, i + by) for i in range(devices) if 0 <= i + by < devices]
    return lax.ppermute(x, axis, pairs)


def extended(x, sides, width):
    for axis, dim in sides:
        devices, length = (lax.axis_size(axis), x.shape[dim])
        up = [(i, (i + 1) % devices) for i in range(devices - 1)]
        down = [(j, i) for i, j in up]
        last = lax.slice_in_dim(x, length - width, length, axis=dim)
        first = lax.slice_in_dim(x, 0, width, axis=dim)
        before = lax.ppermute(last, axis, up)
        after = lax.ppermute(first, axis, down)
        x = jnp.concatenate([before, x, after], axis=dim)
    return x


def activate(volume, gain):
    values = volume.astype(jnp.float32)
    square_mean = jnp.mean(values * values, axis=-1, keepdims=True)
    normed = values * lax.rsqrt(square_mean + 1e-06) * gain
    return jax.nn.silu(normed).astype(jnp.bfloat16)


def make_folder(widened, frames, rows, cols):

    def fold_piece(total, piece, start):
        count_in = piece.shape[1]
        for step_t in range(3):
            for step_h in range(3):
                for step_w in range(3):
                    window = widened[
                        step_t : step_t + frames, step_h : step_h + rows, step_w : step_w + cols
                    ]
                    total = total + jnp.dot(
                        window.reshape(-1, count_in),
                        piece[9 * step_t + 3 * step_h + step_w],
                        preferred_element_type=jnp.float32,
                    )
        return total

    return fold_piece


def convolve(widened, kernel, bias, frames, rows, cols):
    out_chans = kernel.shape[2]
    empty = jnp.zeros((frames * rows * cols, out_chans), jnp.float32)
    fold_piece = make_folder(widened, frames, rows, cols)
    row_kernel = lax.all_gather(kernel, "width", axis=1, tiled=True)
    total = fold_piece(
        empty, lax.all_gather(row_kernel, "height", axis=1, tiled=True), jnp.int32(0)
    )
    return total.reshape(frames, rows, cols, out_chans) + bias


def widen(active):
    earlier = passed_along(active[-2:], "tm", 1)
    tall = jnp.concatenate([earlier, active], axis=0)
    return extended(tall, (("height", 1), ("width", 2)), 1)


def on_device(
    features, first_gain, first_kernel, first_bias, second_gain, second_kernel, second_bias
):
    frames, rows, cols, chans = features.shape
    first_active = activate(features, first_gain)
    middle = convolve(widen(first_active), first_kernel, first_bias, frames, rows, cols).astype(
        jnp.bfloat16
    )
    second_active = activate(middle, second_gain)
    second_wide = widen(second_active)
    summed = convolve(
        second_wide, second_kernel, second_bias, frames, rows, cols
    ) + features.astype(jnp.float32)
    return summed.astype(jnp.bfloat16)


def solution(mesh):
    placed = (
        P("tm", "height", "width", None),
        P(),
        P(None, ("height", "width"), None),
        P(),
        P(),
        P(None, ("height", "width"), None),
        P(),
    )
    return jax.shard_map(
        on_device,
        mesh=mesh,
        in_specs=placed,
        out_specs=P("tm", "height", "width", None),
        check_vma=False,
    )
```

profile of v0, /device:TPU:1, one launch (start us, length us, event | category | flops | bytes accessed | tf_op | source)
XLA Modules:
  0.0 329.2 jit_solution(13650596367216335500)
XLA Ops:
  8.1 45.3 %all-gather.5.cloned.1.call-done = bf16[27,96,384]{2,0,1:T(8,128)(2,1)} async-done(((bf16[27,6,384]{2,0,1:T(8,128)(2,1)}), bf16[27,96,384]{2,0,1:T(8,128)(2,1)}) %all-gather.5.cloned.1.call-update) | async-done | bytes 1990672 | tf_op jit(solution)/shard_map/all_gather | solution.py:57
  53.4 3.7 %copy.15 = bf16[27,96,384]{2,1,0:T(8,128)(2,1)} copy(bf16[27,96,384]{2,0,1:T(8,128)(2,1)} %all-gather.5.cloned.1.call-done) | data formatting | bytes 3981312 | tf_op jit(solution)/shard_map/all_gather | solution.py:57
  57.1 36.5 %all-gather.9.cloned.1.call-done = bf16[27,96,384]{2,0,1:T(8,128)(2,1)} async-done(((bf16[27,6,384]{2,0,1:T(8,128)(2,1)}), bf16[27,96,384]{2,0,1:T(8,128)(2,1)}) %all-gather.9.cloned.1.call-update) | async-done | bytes 1990672 | tf_op jit(solution)/shard_map/all_gather | solution.py:57
  93.6 3.7 %copy.16 = bf16[27,96,384]{2,1,0:T(8,128)(2,1)} copy(bf16[27,96,384]{2,0,1:T(8,128)(2,1)} %all-gather.9.cloned.1.call-done) | data formatting | bytes 3981312 | tf_op jit(solution)/shard_map/all_gather | solution.py:57
  97.9 3.1 collective-permute-start
  101.8 3.2 collective-permute-done
  106.3 4.0 %collective-permute-start.1 = (bf16[6,1,10,384]{3,2,1,0:T(8,128)(2,1)S(1)}, bf16[6,1,10,384]{3,2,1,0:T(8,128)(2,1)S(1)}, u32[]{:S(2)}, u32[]{:S(2)}) collective-permute-start(bf16[6,1,10,384]{3,2,1,0:T(8,128)(2,1)S(1)} %get-tuple-element.71), channel_id=1, source_target_pairs={{0,16},{16,32},{32,48},{1,17},{17,33},{33,49},{2,18},{18,34},{34,5... | collective-permute-start | bytes 138248 | tf_op jit(solution)/shard_map/ppermute | solution.py:20
  114.2 4.9 %collective-permute-start.3 = (bf16[6,10,1,384]{3,2,1,0:T(2,128)(2,1)}, bf16[6,10,1,384]{3,2,1,0:T(2,128)(2,1)S(1)}, u32[]{:S(2)}, u32[]{:S(2)}) collective-permute-start(bf16[6,10,1,384]{3,2,1,0:T(2,128)(2,1)} %get-tuple-element.47), channel_id=1, source_target_pairs={{0,1},{1,2},{2,3},{3,4},{4,5},{5,6},{6,7},{7,8},{8,9},{9,10},{10,1... | collective-permute-start | bytes 138248 | tf_op jit(solution)/shard_map/ppermute | solution.py:20
  119.1 2.1 collective-permute-start.4
  127.2 2.3 fusion.32
  129.4 1.8 reshape.211
  131.2 1.8 reshape.197
  133.0 1.8 reshape.199
  134.8 1.8 reshape.200
  136.6 1.8 reshape.202
  138.4 1.8 reshape.203
  140.2 1.8 reshape.205
  142.0 1.8 reshape.206
  143.8 1.8 reshape.208
  145.6 1.8 reshape.209
  151.7 24.5 %all-gather.7.cloned.1.call-done = bf16[27,384,384]{2,1,0:T(8,128)(2,1)} async-done(((bf16[27,96,384]{2,1,0:T(8,128)(2,1)}), bf16[27,384,384]{2,1,0:T(8,128)(2,1)}) %all-gather.7.cloned.1.call-update) | async-done | bytes 7962640 | tf_op jit(solution)/shard_map/all_gather | solution.py:59
  176.2 1.6 fusion.23
  177.8 1.8 fusion.24
  179.5 1.4 convolution_add_fusion.49
  181.0 1.5 convolution_add_fusion.48
  182.4 1.5 convolution_add_fusion.47
  183.9 1.3 convolution_add_fusion.46
  186.4 1.3 convolution_add_fusion.42
  194.3 3.3 collective-permute-start.5
  197.6 3.5 %collective-permute-done.5 = bf16[2,8,10,384]{3,2,1,0:T(8,128)(2,1)S(1)} collective-permute-done((bf16[2,8,10,384]{3,2,1,0:T(8,128)(2,1)S(1)}, bf16[2,8,10,384]{3,2,1,0:T(8,128)(2,1)S(1)}, u32[]{:S(2)}, u32[]{:S(2)}) %collective-permute-start.5) | collective-permute-done | bytes 122912 | tf_op jit(solution)/shard_map/ppermute | solution.py:10
  202.5 4.2 %collective-permute-start.6 = (bf16[6,1,10,384]{3,2,1,0:T(8,128)(2,1)S(1)}, bf16[6,1,10,384]{3,2,1,0:T(8,128)(2,1)S(1)}, u32[]{:S(2)}, u32[]{:S(2)}) collective-permute-start(bf16[6,1,10,384]{3,2,1,0:T(8,128)(2,1)S(1)} %get-tuple-element.65), channel_id=1, source_target_pairs={{0,16},{16,32},{32,48},{1,17},{17,33},{33,49},{2,18},{18,34},{34,5... | collective-permute-start | bytes 138248 | tf_op jit(solution)/shard_map/ppermute | solution.py:20
  210.1 5.8 %collective-permute-start.8 = (bf16[6,10,1,384]{3,2,1,0:T(2,128)(2,1)}, bf16[6,10,1,384]{3,2,1,0:T(2,128)(2,1)}, u32[]{:S(2)}, u32[]{:S(2)}) collective-permute-start(bf16[6,10,1,384]{3,2,1,0:T(2,128)(2,1)} %get-tuple-element.25), channel_id=1, source_target_pairs={{0,1},{1,2},{2,3},{3,4},{4,5},{5,6},{6,7},{7,8},{8,9},{9,10},{10,1... | collective-permute-start | bytes 138248 | tf_op jit(solution)/shard_map/ppermute | solution.py:20
  215.9 1.9 collective-permute-start.9
  220.1 42.1 %all-gather.11.cloned.1.call-done = bf16[27,384,384]{2,1,0:T(8,128)(2,1)} async-done(((bf16[27,96,384]{2,1,0:T(8,128)(2,1)}), bf16[27,384,384]{2,1,0:T(8,128)(2,1)}) %all-gather.11.cloned.1.call-update) | async-done | bytes 7962640 | tf_op jit(solution)/shard_map/all_gather | solution.py:59
  262.2 1.4 fusion.22
  263.6 1.8 reshape.232
  266.2 1.8 reshape.241
  268.8 1.8 reshape.249
  270.5 1.6 maximum_maximum_fusion.1
  272.1 1.8 fusion.30
  273.9 1.8 reshape.239
  275.7 1.9 fusion.31
  277.6 1.9 reshape.225
  279.4 1.8 reshape.227
  281.2 1.8 reshape.228
  283.0 1.8 reshape.230
  284.8 1.8 reshape.231
  286.6 1.8 reshape.233
  288.4 1.8 reshape.234
  290.1 1.8 reshape.236
  291.9 1.8 reshape.237
  293.7 1.8 reshape.240
  295.5 1.8 reshape.242
  297.3 1.8 reshape.243
  300.3 1.6 fusion.21
  301.9 1.4 convolution_add_fusion.24
  303.3 1.5 convolution_add_fusion.23
  304.8 1.5 convolution_add_fusion.22
  306.2 1.5 convolution_add_fusion.21
  307.7 1.6 convolution_add_fusion.20
  309.3 1.5 convolution_add_fusion.19
  310.8 1.5 convolution_add_fusion.18
  312.2 1.5 convolution_add_fusion.17
  313.7 1.3 convolution_add_fusion.16
  (186 shorter events, 42.7 us)
Async XLA Ops:
  6.5 90.8 %copy-start.1 = (bf16[4,8,10,384]{3,1,2,0:T(8,128)(2,1)S(1)}, bf16[4,8,10,384]{3,1,2,0:T(8,128)(2,1)}, u32[]{:S(2)}) copy-start(bf16[4,8,10,384]{3,1,2,0:T(8,128)(2,1)} %param.7) | copy-start | bytes 737284
  6.5 91.0 %copy-start.35 = (f32[384]{0:T(512)S(1)}, f32[384]{0:T(512)}, u32[]{:S(2)}) copy-start(f32[384]{0:T(512)} %param.8) | copy-start | bytes 4612
  6.5 46.8 %all-gather.5.cloned.1.call-start = ((), (), s32[]{:S(2)}) async-start(), calls=%async_computation | async-start | bytes 2506752 | tf_op jit(solution)/shard_map/all_gather | solution.py:57
  7.3 86.4 %all-gather.9.cloned.1.call-start = ((), (), s32[]{:S(2)}) async-start(), calls=%async_computation.2 | async-start | bytes 2506752 | tf_op jit(solution)/shard_map/all_gather | solution.py:57
  8.0 168.2 %all-gather.7.cloned.1.call-start = ((), (), s32[]{:S(2)}) async-start(), calls=%async_computation.1 | async-start | bytes 9953280 | tf_op jit(solution)/shard_map/all_gather | solution.py:59
  57.1 205.1 %all-gather.11.cloned.1.call-start = ((), (), s32[]{:S(2)}) async-start(), calls=%async_computation.3 | async-start | bytes 9953280 | tf_op jit(solution)/shard_map/all_gather | solution.py:59
  97.9 7.1 %collective-permute-start = (bf16[2,8,10,384]{3,2,1,0:T(8,128)(2,1)S(1)}, bf16[2,8,10,384]{3,2,1,0:T(8,128)(2,1)S(1)}, u32[]{:S(2)}, u32[]{:S(2)}) collective-permute-start(bf16[2,8,10,384]{3,2,1,0:T(8,128)(2,1)S(1)} %slice.512), channel_id=1, source_target_pairs={{0,64},{64,128},{128,192},{1,65},{65,129},{129,193},{2,66},{66,130... | collective-permute-start | bytes 368648 | tf_op jit(solution)/shard_map/ppermute | solution.py:10
  105.0 7.0 %collective-permute-start.2 = (bf16[6,1,10,384]{3,2,1,0:T(8,128)(2,1)S(1)}, bf16[6,1,10,384]{3,2,1,0:T(8,128)(2,1)S(1)}, u32[]{:S(2)}, u32[]{:S(2)}) collective-permute-start(bf16[6,1,10,384]{3,2,1,0:T(8,128)(2,1)S(1)} %get-tuple-element.72), channel_id=1, source_target_pairs={{16,0},{32,16},{48,32},{17,1},{33,17},{49,33},{18,2},{34,18},{50,3... | collective-permute-start | bytes 138248 | tf_op jit(solution)/shard_map/ppermute | solution.py:21
  106.3 7.0 %collective-permute-start.1 = (bf16[6,1,10,384]{3,2,1,0:T(8,128)(2,1)S(1)}, bf16[6,1,10,384]{3,2,1,0:T(8,128)(2,1)S(1)}, u32[]{:S(2)}, u32[]{:S(2)}) collective-permute-start(bf16[6,1,10,384]{3,2,1,0:T(8,128)(2,1)S(1)} %get-tuple-element.71), channel_id=1, source_target_pairs={{0,16},{16,32},{32,48},{1,17},{17,33},{33,49},{2,18},{18,34},{34,5... | collective-permute-start | bytes 138248 | tf_op jit(solution)/shard_map/ppermute | solution.py:20
  114.2 12.3 %collective-permute-start.3 = (bf16[6,10,1,384]{3,2,1,0:T(2,128)(2,1)}, bf16[6,10,1,384]{3,2,1,0:T(2,128)(2,1)S(1)}, u32[]{:S(2)}, u32[]{:S(2)}) collective-permute-start(bf16[6,10,1,384]{3,2,1,0:T(2,128)(2,1)} %get-tuple-element.47), channel_id=1, source_target_pairs={{0,1},{1,2},{2,3},{3,4},{4,5},{5,6},{6,7},{7,8},{8,9},{9,10},{10,1... | collective-permute-start | bytes 138248 | tf_op jit(solution)/shard_map/ppermute | solution.py:20
  119.1 7.4 %collective-permute-start.4 = (bf16[6,10,1,384]{3,2,1,0:T(2,128)(2,1)}, bf16[6,10,1,384]{3,2,1,0:T(2,128)(2,1)S(1)}, u32[]{:S(2)}, u32[]{:S(2)}) collective-permute-start(bf16[6,10,1,384]{3,2,1,0:T(2,128)(2,1)} %get-tuple-element.48), channel_id=1, source_target_pairs={{1,0},{2,1},{3,2},{4,3},{5,4},{6,5},{7,6},{8,7},{9,8},{10,9},{11,1... | collective-permute-start | bytes 138248 | tf_op jit(solution)/shard_map/ppermute | solution.py:21
  148.1 35.8 %copy-start.7 = (bf16[320,384]{1,0:T(8,128)(2,1)S(1)}, bf16[320,384]{1,0:T(8,128)(2,1)}, u32[]{:S(2)}) copy-start(bf16[320,384]{1,0:T(8,128)(2,1)} %reshape.201) | copy-start | bytes 737284
  148.9 37.1 %copy-start.14 = (bf16[320,384]{1,0:T(8,128)(2,1)S(1)}, bf16[320,384]{1,0:T(8,128)(2,1)}, u32[]{:S(2)}) copy-start(bf16[320,384]{1,0:T(8,128)(2,1)} %reshape.204) | copy-start | bytes 737284
  151.4 36.3 %copy-start.26 = (bf16[320,384]{1,0:T(8,128)(2,1)S(1)}, bf16[320,384]{1,0:T(8,128)(2,1)}, u32[]{:S(2)}) copy-start(bf16[320,384]{1,0:T(8,128)(2,1)} %reshape.206) | copy-start | bytes 737284
  151.5 33.8 %copy-start.31 = (bf16[320,384]{1,0:T(8,128)(2,1)S(1)}, bf16[320,384]{1,0:T(8,128)(2,1)}, u32[]{:S(2)}) copy-start(bf16[320,384]{1,0:T(8,128)(2,1)} %reshape.202) | copy-start | bytes 737284
  151.5 34.2 %copy-start.29 = (bf16[320,384]{1,0:T(8,128)(2,1)S(1)}, bf16[320,384]{1,0:T(8,128)(2,1)}, u32[]{:S(2)}) copy-start(bf16[320,384]{1,0:T(8,128)(2,1)} %reshape.203) | copy-start | bytes 737284
  176.2 9.1 %copy-start = (bf16[27,384,384]{2,1,0:T(8,128)(2,1)S(1)}, bf16[27,384,384]{2,1,0:T(8,128)(2,1)}, u32[]{:S(2)}) copy-start(bf16[27,384,384]{2,1,0:T(8,128)(2,1)} %all-gather.7.cloned.1.call-done) | copy-start | bytes 23887876
  176.2 11.9 %copy-start.12 = (bf16[320,384]{1,0:T(8,128)(2,1)S(1)}, bf16[320,384]{1,0:T(8,128)(2,1)}, u32[]{:S(2)}) copy-start(bf16[320,384]{1,0:T(8,128)(2,1)} %reshape.207) | copy-start | bytes 737284
  177.8 10.7 %copy-start.25 = (bf16[320,384]{1,0:T(8,128)(2,1)S(1)}, bf16[320,384]{1,0:T(8,128)(2,1)}, u32[]{:S(2)}) copy-start(bf16[320,384]{1,0:T(8,128)(2,1)} %reshape.208) | copy-start | bytes 737284
  181.0 7.8 %copy-start.23 = (bf16[320,384]{1,0:T(8,128)(2,1)S(1)}, bf16[320,384]{1,0:T(8,128)(2,1)}, u32[]{:S(2)}) copy-start(bf16[320,384]{1,0:T(8,128)(2,1)} %reshape.209) | copy-start | bytes 737284
  182.4 6.7 %copy-start.33 = (bf16[320,384]{1,0:T(8,128)(2,1)S(1)}, bf16[320,384]{1,0:T(8,128)(2,1)}, u32[]{:S(2)}) copy-start(bf16[320,384]{1,0:T(8,128)(2,1)} %reshape.210) | copy-start | bytes 737284
  183.9 5.6 %copy-start.20 = (bf16[320,384]{1,0:T(8,128)(2,1)S(1)}, bf16[320,384]{1,0:T(8,128)(2,1)}, u32[]{:S(2)}) copy-start(bf16[320,384]{1,0:T(8,128)(2,1)} %reshape.212) | copy-start | bytes 737284
  185.3 4.5 %copy-start.10 = (bf16[320,384]{1,0:T(8,128)(2,1)S(1)}, bf16[320,384]{1,0:T(8,128)(2,1)}, u32[]{:S(2)}) copy-start(bf16[320,384]{1,0:T(8,128)(2,1)} %reshape.213) | copy-start | bytes 737284
  185.7 4.5 %copy-start.18 = (bf16[320,384]{1,0:T(8,128)(2,1)S(1)}, bf16[320,384]{1,0:T(8,128)(2,1)}, u32[]{:S(2)}) copy-start(bf16[320,384]{1,0:T(8,128)(2,1)} %reshape.214) | copy-start | bytes 737284
  186.0 4.5 %copy-start.17 = (bf16[320,384]{1,0:T(8,128)(2,1)S(1)}, bf16[320,384]{1,0:T(8,128)(2,1)}, u32[]{:S(2)}) copy-start(bf16[320,384]{1,0:T(8,128)(2,1)} %reshape.215) | copy-start | bytes 737284
  186.4 4.5 %copy-start.8 = (bf16[320,384]{1,0:T(8,128)(2,1)S(1)}, bf16[320,384]{1,0:T(8,128)(2,1)}, u32[]{:S(2)}) copy-start(bf16[320,384]{1,0:T(8,128)(2,1)} %reshape.216) | copy-start | bytes 737284
  187.7 3.5 %copy-start.16 = (bf16[320,384]{1,0:T(8,128)(2,1)S(1)}, bf16[320,384]{1,0:T(8,128)(2,1)}, u32[]{:S(2)}) copy-start(bf16[320,384]{1,0:T(8,128)(2,1)} %reshape.217) | copy-start | bytes 737284
  188.1 3.5 %copy-start.15 = (bf16[320,384]{1,0:T(8,128)(2,1)S(1)}, bf16[320,384]{1,0:T(8,128)(2,1)}, u32[]{:S(2)}) copy-start(bf16[320,384]{1,0:T(8,128)(2,1)} %reshape.218) | copy-start | bytes 737284
  188.4 3.5 %copy-start.4 = (bf16[320,384]{1,0:T(8,128)(2,1)S(1)}, bf16[320,384]{1,0:T(8,128)(2,1)}, u32[]{:S(2)}) copy-start(bf16[320,384]{1,0:T(8,128)(2,1)} %reshape.219) | copy-start | bytes 737284
  189.5 3.5 %copy-start.5 = (bf16[320,384]{1,0:T(8,128)(2,1)S(1)}, bf16[320,384]{1,0:T(8,128)(2,1)}, u32[]{:S(2)}) copy-start(bf16[320,384]{1,0:T(8,128)(2,1)} %reshape.222) | copy-start | bytes 737284
  189.9 3.5 %copy-start.34 = (f32[384]{0:T(512)S(1)}, f32[384]{0:T(512)}, u32[]{:S(2)}) copy-start(f32[384]{0:T(512)} %param.10) | copy-start | bytes 4612
  190.2 3.8 %copy-start.36 = (f32[384]{0:T(512)S(1)}, f32[384]{0:T(512)}, u32[]{:S(2)}) copy-start(f32[384]{0:T(512)} %param.11) | copy-start | bytes 4612
  194.3 6.8 %collective-permute-start.5 = (bf16[2,8,10,384]{3,2,1,0:T(8,128)(2,1)S(1)}, bf16[2,8,10,384]{3,2,1,0:T(8,128)(2,1)S(1)}, u32[]{:S(2)}, u32[]{:S(2)}) collective-permute-start(bf16[2,8,10,384]{3,2,1,0:T(8,128)(2,1)S(1)} %slice.566), channel_id=1, source_target_pairs={{0,64},{64,128},{128,192},{1,65},{65,129},{129,193},{2,66},{66,130... | collective-permute-start | bytes 368648 | tf_op jit(solution)/shard_map/ppermute | solution.py:10
  201.2 7.2 %collective-permute-start.7 = (bf16[6,1,10,384]{3,2,1,0:T(8,128)(2,1)S(1)}, bf16[6,1,10,384]{3,2,1,0:T(8,128)(2,1)S(1)}, u32[]{:S(2)}, u32[]{:S(2)}) collective-permute-start(bf16[6,1,10,384]{3,2,1,0:T(8,128)(2,1)S(1)} %get-tuple-element.66), channel_id=1, source_target_pairs={{16,0},{32,16},{48,32},{17,1},{33,17},{49,33},{18,2},{34,18},{50,3... | collective-permute-start | bytes 138248 | tf_op jit(solution)/shard_map/ppermute | solution.py:21
  202.5 6.8 %collective-permute-start.6 = (bf16[6,1,10,384]{3,2,1,0:T(8,128)(2,1)S(1)}, bf16[6,1,10,384]{3,2,1,0:T(8,128)(2,1)S(1)}, u32[]{:S(2)}, u32[]{:S(2)}) collective-permute-start(bf16[6,1,10,384]{3,2,1,0:T(8,128)(2,1)S(1)} %get-tuple-element.65), channel_id=1, source_target_pairs={{0,16},{16,32},{32,48},{1,17},{17,33},{33,49},{2,18},{18,34},{34,5... | collective-permute-start | bytes 138248 | tf_op jit(solution)/shard_map/ppermute | solution.py:20
  210.1 60.4 %collective-permute-start.8 = (bf16[6,10,1,384]{3,2,1,0:T(2,128)(2,1)}, bf16[6,10,1,384]{3,2,1,0:T(2,128)(2,1)}, u32[]{:S(2)}, u32[]{:S(2)}) collective-permute-start(bf16[6,10,1,384]{3,2,1,0:T(2,128)(2,1)} %get-tuple-element.25), channel_id=1, source_target_pairs={{0,1},{1,2},{2,3},{3,4},{4,5},{5,6},{6,7},{7,8},{8,9},{9,10},{10,1... | collective-permute-start | bytes 138248 | tf_op jit(solution)/shard_map/ppermute | solution.py:20
  215.9 54.6 %collective-permute-start.9 = (bf16[6,10,1,384]{3,2,1,0:T(2,128)(2,1)}, bf16[6,10,1,384]{3,2,1,0:T(2,128)(2,1)}, u32[]{:S(2)}, u32[]{:S(2)}) collective-permute-start(bf16[6,10,1,384]{3,2,1,0:T(2,128)(2,1)} %get-tuple-element.26), channel_id=1, source_target_pairs={{1,0},{2,1},{3,2},{4,3},{5,4},{6,5},{7,6},{8,7},{9,8},{10,9},{11,1... | collective-permute-start | bytes 138248 | tf_op jit(solution)/shard_map/ppermute | solution.py:21
  277.6 22.3 %copy-start.3 = (bf16[4,8,10,384]{3,2,1,0:T(8,128)(2,1)S(1)}, bf16[4,8,10,384]{3,2,1,0:T(8,128)(2,1)}, u32[]{:S(2)}) copy-start(bf16[4,8,10,384]{3,2,1,0:T(8,128)(2,1)} %get-tuple-element.15) | copy-start | bytes 737284
  277.6 22.5 %copy-start.2 = (bf16[4,8,10,384]{3,2,1,0:T(8,128)(2,1)S(1)}, bf16[4,8,10,384]{3,2,1,0:T(8,128)(2,1)}, u32[]{:S(2)}) copy-start(bf16[4,8,10,384]{3,2,1,0:T(8,128)(2,1)} %get-tuple-element.14) | copy-start | bytes 737284
  299.9 13.8 %copy-start.30 = (bf16[320,384]{1,0:T(8,128)(2,1)S(1)}, bf16[320,384]{1,0:T(8,128)(2,1)}, u32[]{:S(2)}) copy-start(bf16[320,384]{1,0:T(8,128)(2,1)} %reshape.234) | copy-start | bytes 737284
  300.1 15.0 %copy-start.13 = (bf16[320,384]{1,0:T(8,128)(2,1)S(1)}, bf16[320,384]{1,0:T(8,128)(2,1)}, u32[]{:S(2)}) copy-start(bf16[320,384]{1,0:T(8,128)(2,1)} %reshape.235) | copy-start | bytes 737284
  300.3 16.1 %slice-start = ((s8[7962624]{0:T(1024)(128)(4,1)}), s8[4194304]{0:T(1024)(128)(4,1)S(1)}, s32[]{:S(2)}) async-start(s8[7962624]{0:T(1024)(128)(4,1)} %bitcast.217), calls=%async_computation.4 | async-start | bytes 8388608
  300.3 16.1 %copy-start.28 = (bf16[320,384]{1,0:T(8,128)(2,1)S(1)}, bf16[320,384]{1,0:T(8,128)(2,1)}, u32[]{:S(2)}) copy-start(bf16[320,384]{1,0:T(8,128)(2,1)} %reshape.236) | copy-start | bytes 737284
  303.3 13.4 %copy-start.27 = (bf16[320,384]{1,0:T(8,128)(2,1)S(1)}, bf16[320,384]{1,0:T(8,128)(2,1)}, u32[]{:S(2)}) copy-start(bf16[320,384]{1,0:T(8,128)(2,1)} %reshape.237) | copy-start | bytes 737284
  304.8 12.3 %copy-start.32 = (bf16[320,384]{1,0:T(8,128)(2,1)S(1)}, bf16[320,384]{1,0:T(8,128)(2,1)}, u32[]{:S(2)}) copy-start(bf16[320,384]{1,0:T(8,128)(2,1)} %reshape.238) | copy-start | bytes 737284
  306.2 11.2 %copy-start.24 = (bf16[320,384]{1,0:T(8,128)(2,1)S(1)}, bf16[320,384]{1,0:T(8,128)(2,1)}, u32[]{:S(2)}) copy-start(bf16[320,384]{1,0:T(8,128)(2,1)} %reshape.240) | copy-start | bytes 737284
  307.7 8.7 %slice-start.1 = ((s8[7962624]{0:T(1024)(128)(4,1)}), s8[3768320]{0:T(1024)(128)(4,1)S(1)}, s32[]{:S(2)}) async-start(s8[7962624]{0:T(1024)(128)(4,1)} %bitcast.217), calls=%async_computation.5 | async-start | bytes 7536640
  307.7 10.1 %copy-start.11 = (bf16[320,384]{1,0:T(8,128)(2,1)S(1)}, bf16[320,384]{1,0:T(8,128)(2,1)}, u32[]{:S(2)}) copy-start(bf16[320,384]{1,0:T(8,128)(2,1)} %reshape.241) | copy-start | bytes 737284
  309.3 8.9 %copy-start.22 = (bf16[320,384]{1,0:T(8,128)(2,1)S(1)}, bf16[320,384]{1,0:T(8,128)(2,1)}, u32[]{:S(2)}) copy-start(bf16[320,384]{1,0:T(8,128)(2,1)} %reshape.242) | copy-start | bytes 737284
  310.8 7.7 %copy-start.21 = (bf16[320,384]{1,0:T(8,128)(2,1)S(1)}, bf16[320,384]{1,0:T(8,128)(2,1)}, u32[]{:S(2)}) copy-start(bf16[320,384]{1,0:T(8,128)(2,1)} %reshape.243) | copy-start | bytes 737284
  312.2 6.6 %copy-start.9 = (bf16[320,384]{1,0:T(8,128)(2,1)S(1)}, bf16[320,384]{1,0:T(8,128)(2,1)}, u32[]{:S(2)}) copy-start(bf16[320,384]{1,0:T(8,128)(2,1)} %reshape.244) | copy-start | bytes 737284
  313.7 5.5 %copy-start.19 = (bf16[320,384]{1,0:T(8,128)(2,1)S(1)}, bf16[320,384]{1,0:T(8,128)(2,1)}, u32[]{:S(2)}) copy-start(bf16[320,384]{1,0:T(8,128)(2,1)} %reshape.245) | copy-start | bytes 737284
  317.8 3.3 copy-start.6
  318.5 3.3 %copy-start.37 = (f32[384]{0:T(512)S(1)}, f32[384]{0:T(512)}, u32[]{:S(2)}) copy-start(f32[384]{0:T(512)} %param.13) | copy-start | bytes 4612
Sparse Core Ops, SparseCore 0:
  9.2 44.1 all-gather.4
  55.2 38.3 all-gather.8
  95.4 80.7 all-gather.6
  177.9 84.2 all-gather.10
where the time goes:
time: 331 us; the launch traced here: 329 us
  waiting for transfers between devices  159 us (48%)
  local copies, waits for them, and re-layouts  79.1 us (24%)
  matrix products  39.5 us (12%)
  starting transfers between devices  32 us (10%)
  between operations  14.3 us (4%)
  other arithmetic  5.48 us (2%)
    all_gather x2, waiting for transfers between devices, convolve(): row_kernel = lax.all_gather(kernel, 'width', axis=1, tiled=True)  81.8 us
    all_gather x2, waiting for transfers between devices, convolve(): lax.all_gather(row_kernel, 'height', axis=1, tiled=True)  66.6 us
    reshape x53, local copies, waits for them, and re-layouts, fold_piece(): window.reshape(-1, count_in)  63 us
    dot_general x54, matrix products, fold_piece(): jnp.dot(window.reshape(-1, count_in), piece[9 * step_t + 3 * step_h + ste...  39.5 us
    ppermute x4, starting transfers between devices, extended(): before = lax.ppermute(last, axis, up)  18.9 us
    slice x6, local copies, waits for them, and re-layouts, fold_piece(): widened[step_t:step_t + frames, step_h:step_h + rows, step_w:step_w + cols]  7.5 us
    all_gather x2, local copies, waits for them, and re-layouts, convolve(): row_kernel = lax.all_gather(kernel, 'width', axis=1, tiled=True)  7.38 us
    ppermute x2, waiting for transfers between devices, passed_along(): return lax.ppermute(x, axis, pairs)  6.76 us
  transfers between devices with their start and end apart: 14, of which 8 were waited for; matrix products, arithmetic and copies ran while one was open for 22% of the time, Pallas kernels for 0%

commit v1 on v0

--- a/solution.py
+++ b/solution.py
@@ -54,7 +54,14 @@
     out_chans = kernel.shape[2]
     empty = jnp.zeros((frames * rows * cols, out_chans), jnp.float32)
     fold_piece = make_folder(widened, frames, rows, cols)
-    row_kernel = lax.all_gather(kernel, "width", axis=1, tiled=True)
+    ring = [kernel]
+    for hop in range(15):
+        ring.append(lax.ppermute(ring[-1], "width", [(dev, (dev + 1) % 16) for dev in range(16)]))
+    row_kernel = jnp.roll(
+        jnp.concatenate(ring[::-1], axis=1),
+        (lax.axis_index("width") + 1) * ring[0].shape[1],
+        axis=1,
+    )
     total = fold_piece(
         empty, lax.all_gather(row_kernel, "height", axis=1, tiled=True), jnp.int32(0)
     )

time: 331 us -> 412 us (1.24)
  local copies, waits for them, and re-layouts: 79.1 us -> 118 us
  waiting for transfers between devices: 159 us -> 178 us
  starting transfers between devices: 32 us -> 42.4 us
  other arithmetic: 5.48 us -> 12.1 us
    ppermute x0 -> x30, waiting for transfers between devices: none -> 169 us  [convolve(): lax.ppermute(ring[-1], 'width', [(dev, (dev + 1) % 16) for dev in range(1...]
    all_gather x2 -> x0, waiting for transfers between devices: 81.8 us -> none  [convolve(): row_kernel = lax.all_gather(kernel, 'width', axis=1, tiled=True)]
    all_gather x2, waiting for transfers between devices: 66.6 us -> 0.02 us  [convolve(): lax.all_gather(row_kernel, 'height', axis=1, tiled=True)]
    concatenate x0 -> x2, local copies, waits for them, and re-layouts: none -> 42.4 us  [convolve(): jnp.concatenate(ring[::-1], axis=1)]
    ppermute x4, starting transfers between devices: 6.61 us -> 16.7 us  [extended(): after = lax.ppermute(first, axis, down)]
    ppermute x4, starting transfers between devices: 18.9 us -> 10.2 us  [extended(): before = lax.ppermute(last, axis, up)]
    ppermute x0 -> x30, starting transfers between devices: none -> 8.08 us  [convolve(): lax.ppermute(ring[-1], 'width', [(dev, (dev + 1) % 16) for dev in range(1...]
    unnamed x80 -> x102, local copies, waits for them, and re-layouts: 0.17 us -> 7.76 us
  transfers between devices with their start and end apart: 14 -> 42, of which waited for: 8 -> 34; matrix products, arithmetic and copies ran while one was open for 22% -> 22% of each run, Pallas kernels for 0% -> 0%
where the time goes in v1:
time: 412 us; the launch traced here: 408 us
  waiting for transfers between devices  178 us (43%)
  local copies, waits for them, and re-layouts  118 us (29%)
  starting transfers between devices  42.4 us (10%)
  matrix products  42 us (10%)
  between operations  14.7 us (4%)
  other arithmetic  12.1 us (3%)
    ppermute x30, waiting for transfers between devices, convolve(): lax.ppermute(ring[-1], 'width', [(dev, (dev + 1) % 16) for dev in range(1...  169 us
    reshape x53, local copies, waits for them, and re-layouts, fold_piece(): window.reshape(-1, count_in)  59.4 us
    concatenate x2, local copies, waits for them, and re-layouts, convolve(): jnp.concatenate(ring[::-1], axis=1)  42.4 us
    dot_general x54, matrix products, fold_piece(): jnp.dot(window.reshape(-1, count_in), piece[9 * step_t + 3 * step_h + ste...  42 us
    ppermute x4, starting transfers between devices, extended(): after = lax.ppermute(first, axis, down)  16.7 us
    ppermute x4, starting transfers between devices, extended(): before = lax.ppermute(last, axis, up)  10.2 us
  transfers between devices with their start and end apart: 42, of which 34 were waited for; matrix products, arithmetic and copies ran while one was open for 22% of the time, Pallas kernels for 0%

profile of v1, /device:TPU:1, one launch (start us, length us, event | category | flops | bytes accessed | tf_op | source)
XLA Modules:
  0.0 407.6 jit_solution(12340169946971443130)
XLA Ops:
  7.5 3.0 collective-permute-start.4
  10.5 2.3 collective-permute-done.4
  12.8 2.5 collective-permute-start.5
  15.3 2.9 collective-permute-done.5
  18.2 1.8 collective-permute-start.6
  20.1 4.1 %collective-permute-done.6 = bf16[27,6,384]{2,1,0:T(8,128)(2,1)S(1)} collective-permute-done((bf16[27,6,384]{2,1,0:T(8,128)(2,1)S(1)}, bf16[27,6,384]{2,1,0:T(8,128)(2,1)S(1)}, u32[]{:S(2)}, u32[]{:S(2)}) %collective-permute-start.6) | collective-permute-done | bytes 124448 | tf_op jit(solution)/shard_map/ppermute | solution.py:59
  24.8 5.3 %collective-permute-done.7 = bf16[27,6,384]{2,1,0:T(8,128)(2,1)S(1)} collective-permute-done((bf16[27,6,384]{2,1,0:T(8,128)(2,1)S(1)}, bf16[27,6,384]{2,1,0:T(8,128)(2,1)S(1)}, u32[]{:S(2)}, u32[]{:S(2)}) %collective-permute-start.7) | collective-permute-done | bytes 124448 | tf_op jit(solution)/shard_map/ppermute | solution.py:59
  30.2 6.0 %collective-permute-done.8 = bf16[27,6,384]{2,1,0:T(8,128)(2,1)S(1)} collective-permute-done((bf16[27,6,384]{2,1,0:T(8,128)(2,1)S(1)}, bf16[27,6,384]{2,1,0:T(8,128)(2,1)S(1)}, u32[]{:S(2)}, u32[]{:S(2)}) %collective-permute-start.8) | collective-permute-done | bytes 124448 | tf_op jit(solution)/shard_map/ppermute | solution.py:59
  36.2 6.0 %collective-permute-done.9 = bf16[27,6,384]{2,1,0:T(8,128)(2,1)S(1)} collective-permute-done((bf16[27,6,384]{2,1,0:T(8,128)(2,1)S(1)}, bf16[27,6,384]{2,1,0:T(8,128)(2,1)S(1)}, u32[]{:S(2)}, u32[]{:S(2)}) %collective-permute-start.9) | collective-permute-done | bytes 124448 | tf_op jit(solution)/shard_map/ppermute | solution.py:59
  42.1 6.0 %collective-permute-done.10 = bf16[27,6,384]{2,1,0:T(8,128)(2,1)S(1)} collective-permute-done((bf16[27,6,384]{2,1,0:T(8,128)(2,1)S(1)}, bf16[27,6,384]{2,1,0:T(8,128)(2,1)S(1)}, u32[]{:S(2)}, u32[]{:S(2)}) %collective-permute-start.10) | collective-permute-done | bytes 124448 | tf_op jit(solution)/shard_map/ppermute | solution.py:59
  48.1 6.0 %collective-permute-done.11 = bf16[27,6,384]{2,1,0:T(8,128)(2,1)S(1)} collective-permute-done((bf16[27,6,384]{2,1,0:T(8,128)(2,1)S(1)}, bf16[27,6,384]{2,1,0:T(8,128)(2,1)S(1)}, u32[]{:S(2)}, u32[]{:S(2)}) %collective-permute-start.11) | collective-permute-done | bytes 124448 | tf_op jit(solution)/shard_map/ppermute | solution.py:59
  54.8 6.0 %collective-permute-done.12 = bf16[27,6,384]{2,1,0:T(8,128)(2,1)S(1)} collective-permute-done((bf16[27,6,384]{2,1,0:T(8,128)(2,1)S(1)}, bf16[27,6,384]{2,1,0:T(8,128)(2,1)S(1)}, u32[]{:S(2)}, u32[]{:S(2)}) %collective-permute-start.12) | collective-permute-done | bytes 124448 | tf_op jit(solution)/shard_map/ppermute | solution.py:59
  61.4 6.0 %collective-permute-done.13 = bf16[27,6,384]{2,1,0:T(8,128)(2,1)S(1)} collective-permute-done((bf16[27,6,384]{2,1,0:T(8,128)(2,1)S(1)}, bf16[27,6,384]{2,1,0:T(8,128)(2,1)S(1)}, u32[]{:S(2)}, u32[]{:S(2)}) %collective-permute-start.13) | collective-permute-done | bytes 124448 | tf_op jit(solution)/shard_map/ppermute | solution.py:59
  68.0 6.0 %collective-permute-done.14 = bf16[27,6,384]{2,1,0:T(8,128)(2,1)S(1)} collective-permute-done((bf16[27,6,384]{2,1,0:T(8,128)(2,1)S(1)}, bf16[27,6,384]{2,1,0:T(8,128)(2,1)S(1)}, u32[]{:S(2)}, u32[]{:S(2)}) %collective-permute-start.14) | collective-permute-done | bytes 124448 | tf_op jit(solution)/shard_map/ppermute | solution.py:59
  74.7 6.0 %collective-permute-done.15 = bf16[27,6,384]{2,1,0:T(8,128)(2,1)S(1)} collective-permute-done((bf16[27,6,384]{2,1,0:T(8,128)(2,1)S(1)}, bf16[27,6,384]{2,1,0:T(8,128)(2,1)S(1)}, u32[]{:S(2)}, u32[]{:S(2)}) %collective-permute-start.15) | collective-permute-done | bytes 124448 | tf_op jit(solution)/shard_map/ppermute | solution.py:59
  81.3 6.0 %collective-permute-done.16 = bf16[27,6,384]{2,1,0:T(8,128)(2,1)S(1)} collective-permute-done((bf16[27,6,384]{2,1,0:T(8,128)(2,1)S(1)}, bf16[27,6,384]{2,1,0:T(8,128)(2,1)S(1)}, u32[]{:S(2)}, u32[]{:S(2)}) %collective-permute-start.16) | collective-permute-done | bytes 124448 | tf_op jit(solution)/shard_map/ppermute | solution.py:59
  88.0 6.0 %collective-permute-done.17 = bf16[27,6,384]{2,1,0:T(8,128)(2,1)S(1)} collective-permute-done((bf16[27,6,384]{2,1,0:T(8,128)(2,1)S(1)}, bf16[27,6,384]{2,1,0:T(8,128)(2,1)S(1)}, u32[]{:S(2)}, u32[]{:S(2)}) %collective-permute-start.17) | collective-permute-done | bytes 124448 | tf_op jit(solution)/shard_map/ppermute | solution.py:59
  94.6 5.4 %collective-permute-done.18 = bf16[27,6,384]{2,1,0:T(8,128)(2,1)} collective-permute-done((bf16[27,6,384]{2,1,0:T(8,128)(2,1)S(1)}, bf16[27,6,384]{2,1,0:T(8,128)(2,1)}, u32[]{:S(2)}, u32[]{:S(2)}) %collective-permute-start.18) | collective-permute-done | bytes 124448 | tf_op jit(solution)/shard_map/ppermute | solution.py:59
  100.1 20.9 %concatenate.90 = bf16[27,96,384]{2,1,0:T(8,128)(2,1)S(1)} concatenate(bf16[27,6,384]{2,1,0:T(8,128)(2,1)} %collective-permute-done.18, bf16[27,6,384]{2,1,0:T(8,128)(2,1)} %copy-done.37, bf16[27,6,384]{2,1,0:T(8,128)(2,1)} %copy-done.35, bf16[27,6,384]{2,1,0:T(8,128)(2,1)} %copy-done.33, bf16[27,6,384]{2,1,0:T(8,128)(2,1)} %copy-done.32, bf16[27,6,384]{2,1,0:T(8,128)(2,1)} %copy-done.31, ...), dimensions={1} | concatenate | bytes 3981312 | tf_op jit(solution)/shard_map/concatenate | solution.py:61
  120.9 2.8 fusion.1
  124.9 5.9 %collective-permute-done.24 = bf16[27,6,384]{2,1,0:T(8,128)(2,1)S(1)} collective-permute-done((bf16[27,6,384]{2,1,0:T(8,128)(2,1)S(1)}, bf16[27,6,384]{2,1,0:T(8,128)(2,1)S(1)}, u32[]{:S(2)}, u32[]{:S(2)}) %collective-permute-start.24) | collective-permute-done | bytes 124448 | tf_op jit(solution)/shard_map/ppermute | solution.py:59
  130.8 6.0 %collective-permute-done.25 = bf16[27,6,384]{2,1,0:T(8,128)(2,1)S(1)} collective-permute-done((bf16[27,6,384]{2,1,0:T(8,128)(2,1)S(1)}, bf16[27,6,384]{2,1,0:T(8,128)(2,1)S(1)}, u32[]{:S(2)}, u32[]{:S(2)}) %collective-permute-start.25) | collective-permute-done | bytes 124448 | tf_op jit(solution)/shard_map/ppermute | solution.py:59
  136.8 6.0 %collective-permute-done.26 = bf16[27,6,384]{2,1,0:T(8,128)(2,1)S(1)} collective-permute-done((bf16[27,6,384]{2,1,0:T(8,128)(2,1)S(1)}, bf16[27,6,384]{2,1,0:T(8,128)(2,1)S(1)}, u32[]{:S(2)}, u32[]{:S(2)}) %collective-permute-start.26) | collective-permute-done | bytes 124448 | tf_op jit(solution)/shard_map/ppermute | solution.py:59
  142.8 6.0 %collective-permute-done.27 = bf16[27,6,384]{2,1,0:T(8,128)(2,1)S(1)} collective-permute-done((bf16[27,6,384]{2,1,0:T(8,128)(2,1)S(1)}, bf16[27,6,384]{2,1,0:T(8,128)(2,1)S(1)}, u32[]{:S(2)}, u32[]{:S(2)}) %collective-permute-start.27) | collective-permute-done | bytes 124448 | tf_op jit(solution)/shard_map/ppermute | solution.py:59
  148.7 6.0 %collective-permute-done.28 = bf16[27,6,384]{2,1,0:T(8,128)(2,1)S(1)} collective-permute-done((bf16[27,6,384]{2,1,0:T(8,128)(2,1)S(1)}, bf16[27,6,384]{2,1,0:T(8,128)(2,1)S(1)}, u32[]{:S(2)}, u32[]{:S(2)}) %collective-permute-start.28) | collective-permute-done | bytes 124448 | tf_op jit(solution)/shard_map/ppermute | solution.py:59
  154.7 6.0 %collective-permute-done.29 = bf16[27,6,384]{2,1,0:T(8,128)(2,1)S(1)} collective-permute-done((bf16[27,6,384]{2,1,0:T(8,128)(2,1)S(1)}, bf16[27,6,384]{2,1,0:T(8,128)(2,1)S(1)}, u32[]{:S(2)}, u32[]{:S(2)}) %collective-permute-start.29) | collective-permute-done | bytes 124448 | tf_op jit(solution)/shard_map/ppermute | solution.py:59
  160.7 6.0 %collective-permute-done.30 = bf16[27,6,384]{2,1,0:T(8,128)(2,1)S(1)} collective-permute-done((bf16[27,6,384]{2,1,0:T(8,128)(2,1)S(1)}, bf16[27,6,384]{2,1,0:T(8,128)(2,1)S(1)}, u32[]{:S(2)}, u32[]{:S(2)}) %collective-permute-start.30) | collective-permute-done | bytes 124448 | tf_op jit(solution)/shard_map/ppermute | solution.py:59
  166.7 6.0 %collective-permute-done.31 = bf16[27,6,384]{2,1,0:T(8,128)(2,1)S(1)} collective-permute-done((bf16[27,6,384]{2,1,0:T(8,128)(2,1)S(1)}, bf16[27,6,384]{2,1,0:T(8,128)(2,1)S(1)}, u32[]{:S(2)}, u32[]{:S(2)}) %collective-permute-start.31) | collective-permute-done | bytes 124448 | tf_op jit(solution)/shard_map/ppermute | solution.py:59
  172.6 6.0 %collective-permute-done.32 = bf16[27,6,384]{2,1,0:T(8,128)(2,1)S(1)} collective-permute-done((bf16[27,6,384]{2,1,0:T(8,128)(2,1)S(1)}, bf16[27,6,384]{2,1,0:T(8,128)(2,1)S(1)}, u32[]{:S(2)}, u32[]{:S(2)}) %collective-permute-start.32) | collective-permute-done | bytes 124448 | tf_op jit(solution)/shard_map/ppermute | solution.py:59
  178.6 6.0 %collective-permute-done.33 = bf16[27,6,384]{2,1,0:T(8,128)(2,1)S(1)} collective-permute-done((bf16[27,6,384]{2,1,0:T(8,128)(2,1)S(1)}, bf16[27,6,384]{2,1,0:T(8,128)(2,1)S(1)}, u32[]{:S(2)}, u32[]{:S(2)}) %collective-permute-start.33) | collective-permute-done | bytes 124448 | tf_op jit(solution)/shard_map/ppermute | solution.py:59
  184.6 6.0 %collective-permute-done.34 = bf16[27,6,384]{2,1,0:T(8,128)(2,1)S(1)} collective-permute-done((bf16[27,6,384]{2,1,0:T(8,128)(2,1)S(1)}, bf16[27,6,384]{2,1,0:T(8,128)(2,1)S(1)}, u32[]{:S(2)}, u32[]{:S(2)}) %collective-permute-start.34) | collective-permute-done | bytes 124448 | tf_op jit(solution)/shard_map/ppermute | solution.py:59
  190.6 6.0 %collective-permute-done.35 = bf16[27,6,384]{2,1,0:T(8,128)(2,1)S(1)} collective-permute-done((bf16[27,6,384]{2,1,0:T(8,128)(2,1)S(1)}, bf16[27,6,384]{2,1,0:T(8,128)(2,1)S(1)}, u32[]{:S(2)}, u32[]{:S(2)}) %collective-permute-start.35) | collective-permute-done | bytes 124448 | tf_op jit(solution)/shard_map/ppermute | solution.py:59
  196.6 6.0 %collective-permute-done.36 = bf16[27,6,384]{2,1,0:T(8,128)(2,1)S(1)} collective-permute-done((bf16[27,6,384]{2,1,0:T(8,128)(2,1)S(1)}, bf16[27,6,384]{2,1,0:T(8,128)(2,1)S(1)}, u32[]{:S(2)}, u32[]{:S(2)}) %collective-permute-start.36) | collective-permute-done | bytes 124448 | tf_op jit(solution)/shard_map/ppermute | solution.py:59
  202.5 6.0 %collective-permute-done.37 = bf16[27,6,384]{2,1,0:T(8,128)(2,1)S(1)} collective-permute-done((bf16[27,6,384]{2,1,0:T(8,128)(2,1)S(1)}, bf16[27,6,384]{2,1,0:T(8,128)(2,1)S(1)}, u32[]{:S(2)}, u32[]{:S(2)}) %collective-permute-start.37) | collective-permute-done | bytes 124448 | tf_op jit(solution)/shard_map/ppermute | solution.py:59
  209.2 5.4 %collective-permute-done.38 = bf16[27,6,384]{2,1,0:T(8,128)(2,1)} collective-permute-done((bf16[27,6,384]{2,1,0:T(8,128)(2,1)S(1)}, bf16[27,6,384]{2,1,0:T(8,128)(2,1)}, u32[]{:S(2)}, u32[]{:S(2)}) %collective-permute-start.38) | collective-permute-done | bytes 124448 | tf_op jit(solution)/shard_map/ppermute | solution.py:59
  214.6 21.5 %concatenate.97 = bf16[27,96,384]{2,1,0:T(8,128)(2,1)S(1)} concatenate(bf16[27,6,384]{2,1,0:T(8,128)(2,1)} %collective-permute-done.38, bf16[27,6,384]{2,1,0:T(8,128)(2,1)} %copy-done.43, bf16[27,6,384]{2,1,0:T(8,128)(2,1)} %copy-done.42, bf16[27,6,384]{2,1,0:T(8,128)(2,1)} %copy-done.41, bf16[27,6,384]{2,1,0:T(8,128)(2,1)} %copy-done.40, bf16[27,6,384]{2,1,0:T(8,128)(2,1)} %copy-done.39, ...), dimensions={1} | concatenate | bytes 3981312 | tf_op jit(solution)/shard_map/concatenate | solution.py:61
  236.1 2.9 fusion
  239.6 3.2 collective-permute-start
  245.4 3.1 collective-permute-start.1
  251.6 2.1 collective-permute-done.2
  254.5 9.2 %collective-permute-start.19 = (bf16[6,10,1,384]{3,2,1,0:T(2,128)(2,1)}, bf16[6,10,1,384]{3,2,1,0:T(2,128)(2,1)S(1)}, u32[]{:S(2)}, u32[]{:S(2)}) collective-permute-start(bf16[6,10,1,384]{3,2,1,0:T(2,128)(2,1)} %get-tuple-element.49), channel_id=1, source_target_pairs={{1,0},{2,1},{3,2},{4,3},{5,4},{6,5},{7,6},{8,7},{9,8},{10,9},{11,1... | collective-permute-start | bytes 138248 | tf_op jit(solution)/shard_map/ppermute | solution.py:21
  263.7 2.1 collective-permute-start.3
  271.8 2.3 fusion.34
  274.1 1.8 reshape.197
  275.9 1.8 reshape.199
  277.7 1.8 reshape.200
  281.2 1.8 reshape.203
  284.8 1.8 reshape.206
  288.4 1.8 reshape.209
  295.8 2.2 fusion.25
  314.7 4.1 %collective-permute-start.20 = (bf16[2,8,10,384]{3,2,1,0:T(8,128)(2,1)S(1)}, bf16[2,8,10,384]{3,2,1,0:T(8,128)(2,1)S(1)}, u32[]{:S(2)}, u32[]{:S(2)}) collective-permute-start(bf16[2,8,10,384]{3,2,1,0:T(8,128)(2,1)S(1)} %slice.566), channel_id=1, source_target_pairs={{0,64},{64,128},{128,192},{1,65},{65,129},{129,193},{2,66},{66,130... | collective-permute-start | bytes 368648 | tf_op jit(solution)/shard_map/ppermute | solution.py:10
  318.8 3.7 collective-permute-done.20
  322.6 3.1 collective-permute-start.21
  328.9 1.9 collective-permute-done.22
  333.2 1.9 collective-permute-start.23
  335.2 4.7 %collective-permute-start.39 = (bf16[6,10,1,384]{3,2,1,0:T(2,128)(2,1)}, bf16[6,10,1,384]{3,2,1,0:T(2,128)(2,1)}, u32[]{:S(2)}, u32[]{:S(2)}) collective-permute-start(bf16[6,10,1,384]{3,2,1,0:T(2,128)(2,1)} %get-tuple-element.27), channel_id=1, source_target_pairs={{1,0},{2,1},{3,2},{4,3},{5,4},{6,5},{7,6},{8,7},{9,8},{10,9},{11,1... | collective-permute-start | bytes 138248 | tf_op jit(solution)/shard_map/ppermute | solution.py:21
  344.8 1.8 reshape.241
  347.4 1.8 reshape.249
  352.4 1.8 reshape.225
  354.2 2.0 fusion.32
  356.3 1.9 reshape.227
  358.1 1.8 reshape.228
  363.5 1.8 reshape.233
  368.8 1.8 reshape.237
  (264 shorter events, 99.5 us)
Async XLA Ops:
  6.5 287.6 %all-gather.3.cloned.1.call-start = ((), (), s32[]{:S(2)}) async-start(), calls=%async_computation | async-start | bytes 9953280 | tf_op jit(solution)/shard_map/all_gather | solution.py:66
  7.5 5.3 %collective-permute-start.4 = (bf16[27,6,384]{2,1,0:T(8,128)(2,1)S(1)}, bf16[27,6,384]{2,1,0:T(8,128)(2,1)S(1)}, u32[]{:S(2)}, u32[]{:S(2)}) collective-permute-start(bf16[27,6,384]{2,1,0:T(8,128)(2,1)S(1)} %copy.11), channel_id=1, source_target_pairs={{0,1},{1,2},{2,3},{3,4},{4,5},{5,6},{6,7},{7,8},{8,9},{9,10},{10,1... | collective-permute-start | bytes 373256 | tf_op jit(solution)/shard_map/ppermute | solution.py:59
  12.8 5.4 %collective-permute-start.5 = (bf16[27,6,384]{2,1,0:T(8,128)(2,1)S(1)}, bf16[27,6,384]{2,1,0:T(8,128)(2,1)S(1)}, u32[]{:S(2)}, u32[]{:S(2)}) collective-permute-start(bf16[27,6,384]{2,1,0:T(8,128)(2,1)S(1)} %collective-permute-done.4), channel_id=1, source_target_pairs={{0,1},{1,2},{2,3},{3,4},{4,5},{5,6},{6,7},{7,8},{8,9},{9,10},{10,1... | collective-permute-start | bytes 373256 | tf_op jit(solution)/shard_map/ppermute | solution.py:59
  18.2 6.0 %collective-permute-start.6 = (bf16[27,6,384]{2,1,0:T(8,128)(2,1)S(1)}, bf16[27,6,384]{2,1,0:T(8,128)(2,1)S(1)}, u32[]{:S(2)}, u32[]{:S(2)}) collective-permute-start(bf16[27,6,384]{2,1,0:T(8,128)(2,1)S(1)} %collective-permute-done.5), channel_id=1, source_target_pairs={{0,1},{1,2},{2,3},{3,4},{4,5},{5,6},{6,7},{7,8},{8,9},{9,10},{10,1... | collective-permute-start | bytes 373256 | tf_op jit(solution)/shard_map/ppermute | solution.py:59
  24.2 6.0 %collective-permute-start.7 = (bf16[27,6,384]{2,1,0:T(8,128)(2,1)S(1)}, bf16[27,6,384]{2,1,0:T(8,128)(2,1)S(1)}, u32[]{:S(2)}, u32[]{:S(2)}) collective-permute-start(bf16[27,6,384]{2,1,0:T(8,128)(2,1)S(1)} %collective-permute-done.6), channel_id=1, source_target_pairs={{0,1},{1,2},{2,3},{3,4},{4,5},{5,6},{6,7},{7,8},{8,9},{9,10},{10,1... | collective-permute-start | bytes 373256 | tf_op jit(solution)/shard_map/ppermute | solution.py:59
  30.2 6.0 %collective-permute-start.8 = (bf16[27,6,384]{2,1,0:T(8,128)(2,1)S(1)}, bf16[27,6,384]{2,1,0:T(8,128)(2,1)S(1)}, u32[]{:S(2)}, u32[]{:S(2)}) collective-permute-start(bf16[27,6,384]{2,1,0:T(8,128)(2,1)S(1)} %collective-permute-done.7), channel_id=1, source_target_pairs={{0,1},{1,2},{2,3},{3,4},{4,5},{5,6},{6,7},{7,8},{8,9},{9,10},{10,1... | collective-permute-start | bytes 373256 | tf_op jit(solution)/shard_map/ppermute | solution.py:59
  36.2 6.0 %collective-permute-start.9 = (bf16[27,6,384]{2,1,0:T(8,128)(2,1)S(1)}, bf16[27,6,384]{2,1,0:T(8,128)(2,1)S(1)}, u32[]{:S(2)}, u32[]{:S(2)}) collective-permute-start(bf16[27,6,384]{2,1,0:T(8,128)(2,1)S(1)} %collective-permute-done.8), channel_id=1, source_target_pairs={{0,1},{1,2},{2,3},{3,4},{4,5},{5,6},{6,7},{7,8},{8,9},{9,10},{10,1... | collective-permute-start | bytes 373256 | tf_op jit(solution)/shard_map/ppermute | solution.py:59
  42.1 6.0 %collective-permute-start.10 = (bf16[27,6,384]{2,1,0:T(8,128)(2,1)S(1)}, bf16[27,6,384]{2,1,0:T(8,128)(2,1)S(1)}, u32[]{:S(2)}, u32[]{:S(2)}) collective-permute-start(bf16[27,6,384]{2,1,0:T(8,128)(2,1)S(1)} %collective-permute-done.9), channel_id=1, source_target_pairs={{0,1},{1,2},{2,3},{3,4},{4,5},{5,6},{6,7},{7,8},{8,9},{9,10},{10,1... | collective-permute-start | bytes 373256 | tf_op jit(solution)/shard_map/ppermute | solution.py:59
  48.1 6.0 %collective-permute-start.11 = (bf16[27,6,384]{2,1,0:T(8,128)(2,1)S(1)}, bf16[27,6,384]{2,1,0:T(8,128)(2,1)S(1)}, u32[]{:S(2)}, u32[]{:S(2)}) collective-permute-start(bf16[27,6,384]{2,1,0:T(8,128)(2,1)S(1)} %collective-permute-done.10), channel_id=1, source_target_pairs={{0,1},{1,2},{2,3},{3,4},{4,5},{5,6},{6,7},{7,8},{8,9},{9,10},{10,1... | collective-permute-start | bytes 373256 | tf_op jit(solution)/shard_map/ppermute | solution.py:59
  54.8 6.0 %collective-permute-start.12 = (bf16[27,6,384]{2,1,0:T(8,128)(2,1)S(1)}, bf16[27,6,384]{2,1,0:T(8,128)(2,1)S(1)}, u32[]{:S(2)}, u32[]{:S(2)}) collective-permute-start(bf16[27,6,384]{2,1,0:T(8,128)(2,1)S(1)} %collective-permute-done.11), channel_id=1, source_target_pairs={{0,1},{1,2},{2,3},{3,4},{4,5},{5,6},{6,7},{7,8},{8,9},{9,10},{10,1... | collective-permute-start | bytes 373256 | tf_op jit(solution)/shard_map/ppermute | solution.py:59
  61.4 6.0 %collective-permute-start.13 = (bf16[27,6,384]{2,1,0:T(8,128)(2,1)S(1)}, bf16[27,6,384]{2,1,0:T(8,128)(2,1)S(1)}, u32[]{:S(2)}, u32[]{:S(2)}) collective-permute-start(bf16[27,6,384]{2,1,0:T(8,128)(2,1)S(1)} %collective-permute-done.12), channel_id=1, source_target_pairs={{0,1},{1,2},{2,3},{3,4},{4,5},{5,6},{6,7},{7,8},{8,9},{9,10},{10,1... | collective-permute-start | bytes 373256 | tf_op jit(solution)/shard_map/ppermute | solution.py:59
  68.0 6.0 %collective-permute-start.14 = (bf16[27,6,384]{2,1,0:T(8,128)(2,1)S(1)}, bf16[27,6,384]{2,1,0:T(8,128)(2,1)S(1)}, u32[]{:S(2)}, u32[]{:S(2)}) collective-permute-start(bf16[27,6,384]{2,1,0:T(8,128)(2,1)S(1)} %collective-permute-done.13), channel_id=1, source_target_pairs={{0,1},{1,2},{2,3},{3,4},{4,5},{5,6},{6,7},{7,8},{8,9},{9,10},{10,1... | collective-permute-start | bytes 373256 | tf_op jit(solution)/shard_map/ppermute | solution.py:59
  74.7 6.0 %collective-permute-start.15 = (bf16[27,6,384]{2,1,0:T(8,128)(2,1)S(1)}, bf16[27,6,384]{2,1,0:T(8,128)(2,1)S(1)}, u32[]{:S(2)}, u32[]{:S(2)}) collective-permute-start(bf16[27,6,384]{2,1,0:T(8,128)(2,1)S(1)} %collective-permute-done.14), channel_id=1, source_target_pairs={{0,1},{1,2},{2,3},{3,4},{4,5},{5,6},{6,7},{7,8},{8,9},{9,10},{10,1... | collective-permute-start | bytes 373256 | tf_op jit(solution)/shard_map/ppermute | solution.py:59
  81.3 6.0 %collective-permute-start.16 = (bf16[27,6,384]{2,1,0:T(8,128)(2,1)S(1)}, bf16[27,6,384]{2,1,0:T(8,128)(2,1)S(1)}, u32[]{:S(2)}, u32[]{:S(2)}) collective-permute-start(bf16[27,6,384]{2,1,0:T(8,128)(2,1)S(1)} %collective-permute-done.15), channel_id=1, source_target_pairs={{0,1},{1,2},{2,3},{3,4},{4,5},{5,6},{6,7},{7,8},{8,9},{9,10},{10,1... | collective-permute-start | bytes 373256 | tf_op jit(solution)/shard_map/ppermute | solution.py:59
  88.0 6.0 %collective-permute-start.17 = (bf16[27,6,384]{2,1,0:T(8,128)(2,1)S(1)}, bf16[27,6,384]{2,1,0:T(8,128)(2,1)S(1)}, u32[]{:S(2)}, u32[]{:S(2)}) collective-permute-start(bf16[27,6,384]{2,1,0:T(8,128)(2,1)S(1)} %collective-permute-done.16), channel_id=1, source_target_pairs={{0,1},{1,2},{2,3},{3,4},{4,5},{5,6},{6,7},{7,8},{8,9},{9,10},{10,1... | collective-permute-start | bytes 373256 | tf_op jit(solution)/shard_map/ppermute | solution.py:59
  93.9 6.1 %collective-permute-start.18 = (bf16[27,6,384]{2,1,0:T(8,128)(2,1)S(1)}, bf16[27,6,384]{2,1,0:T(8,128)(2,1)}, u32[]{:S(2)}, u32[]{:S(2)}) collective-permute-start(bf16[27,6,384]{2,1,0:T(8,128)(2,1)S(1)} %collective-permute-done.17), channel_id=1, source_target_pairs={{0,1},{1,2},{2,3},{3,4},{4,5},{5,6},{6,7},{7,8},{8,9},{9,10},{10,1... | collective-permute-start | bytes 373256 | tf_op jit(solution)/shard_map/ppermute | solution.py:59
  120.9 118.1 %copy-start.1 = (bf16[4,8,10,384]{3,1,2,0:T(8,128)(2,1)S(1)}, bf16[4,8,10,384]{3,1,2,0:T(8,128)(2,1)}, u32[]{:S(2)}) copy-start(bf16[4,8,10,384]{3,1,2,0:T(8,128)(2,1)} %param.9) | copy-start | bytes 737284
  120.9 118.3 %copy-start.45 = (f32[384]{0:T(512)S(1)}, f32[384]{0:T(512)}, u32[]{:S(2)}) copy-start(f32[384]{0:T(512)} %param.10) | copy-start | bytes 4612
  123.8 217.1 %all-gather.5.cloned.1.call-start = ((), (), s32[]{:S(2)}) async-start(), calls=%async_computation.1 | async-start | bytes 9953280 | tf_op jit(solution)/shard_map/all_gather | solution.py:66
  124.8 6.0 %collective-permute-start.24 = (bf16[27,6,384]{2,1,0:T(8,128)(2,1)S(1)}, bf16[27,6,384]{2,1,0:T(8,128)(2,1)S(1)}, u32[]{:S(2)}, u32[]{:S(2)}) collective-permute-start(bf16[27,6,384]{2,1,0:T(8,128)(2,1)S(1)} %copy.13), channel_id=1, source_target_pairs={{0,1},{1,2},{2,3},{3,4},{4,5},{5,6},{6,7},{7,8},{8,9},{9,10},{10,1... | collective-permute-start | bytes 373256 | tf_op jit(solution)/shard_map/ppermute | solution.py:59
  130.8 6.0 %collective-permute-start.25 = (bf16[27,6,384]{2,1,0:T(8,128)(2,1)S(1)}, bf16[27,6,384]{2,1,0:T(8,128)(2,1)S(1)}, u32[]{:S(2)}, u32[]{:S(2)}) collective-permute-start(bf16[27,6,384]{2,1,0:T(8,128)(2,1)S(1)} %collective-permute-done.24), channel_id=1, source_target_pairs={{0,1},{1,2},{2,3},{3,4},{4,5},{5,6},{6,7},{7,8},{8,9},{9,10},{10,1... | collective-permute-start | bytes 373256 | tf_op jit(solution)/shard_map/ppermute | solution.py:59
  136.8 6.0 %collective-permute-start.26 = (bf16[27,6,384]{2,1,0:T(8,128)(2,1)S(1)}, bf16[27,6,384]{2,1,0:T(8,128)(2,1)S(1)}, u32[]{:S(2)}, u32[]{:S(2)}) collective-permute-start(bf16[27,6,384]{2,1,0:T(8,128)(2,1)S(1)} %collective-permute-done.25), channel_id=1, source_target_pairs={{0,1},{1,2},{2,3},{3,4},{4,5},{5,6},{6,7},{7,8},{8,9},{9,10},{10,1... | collective-permute-start | bytes 373256 | tf_op jit(solution)/shard_map/ppermute | solution.py:59
  142.7 6.0 %collective-permute-start.27 = (bf16[27,6,384]{2,1,0:T(8,128)(2,1)S(1)}, bf16[27,6,384]{2,1,0:T(8,128)(2,1)S(1)}, u32[]{:S(2)}, u32[]{:S(2)}) collective-permute-start(bf16[27,6,384]{2,1,0:T(8,128)(2,1)S(1)} %collective-permute-done.26), channel_id=1, source_target_pairs={{0,1},{1,2},{2,3},{3,4},{4,5},{5,6},{6,7},{7,8},{8,9},{9,10},{10,1... | collective-permute-start | bytes 373256 | tf_op jit(solution)/shard_map/ppermute | solution.py:59
  148.7 6.0 %collective-permute-start.28 = (bf16[27,6,384]{2,1,0:T(8,128)(2,1)S(1)}, bf16[27,6,384]{2,1,0:T(8,128)(2,1)S(1)}, u32[]{:S(2)}, u32[]{:S(2)}) collective-permute-start(bf16[27,6,384]{2,1,0:T(8,128)(2,1)S(1)} %collective-permute-done.27), channel_id=1, source_target_pairs={{0,1},{1,2},{2,3},{3,4},{4,5},{5,6},{6,7},{7,8},{8,9},{9,10},{10,1... | collective-permute-start | bytes 373256 | tf_op jit(solution)/shard_map/ppermute | solution.py:59
  154.7 6.0 %collective-permute-start.29 = (bf16[27,6,384]{2,1,0:T(8,128)(2,1)S(1)}, bf16[27,6,384]{2,1,0:T(8,128)(2,1)S(1)}, u32[]{:S(2)}, u32[]{:S(2)}) collective-permute-start(bf16[27,6,384]{2,1,0:T(8,128)(2,1)S(1)} %collective-permute-done.28), channel_id=1, source_target_pairs={{0,1},{1,2},{2,3},{3,4},{4,5},{5,6},{6,7},{7,8},{8,9},{9,10},{10,1... | collective-permute-start | bytes 373256 | tf_op jit(solution)/shard_map/ppermute | solution.py:59
  160.7 6.0 %collective-permute-start.30 = (bf16[27,6,384]{2,1,0:T(8,128)(2,1)S(1)}, bf16[27,6,384]{2,1,0:T(8,128)(2,1)S(1)}, u32[]{:S(2)}, u32[]{:S(2)}) collective-permute-start(bf16[27,6,384]{2,1,0:T(8,128)(2,1)S(1)} %collective-permute-done.29), channel_id=1, source_target_pairs={{0,1},{1,2},{2,3},{3,4},{4,5},{5,6},{6,7},{7,8},{8,9},{9,10},{10,1... | collective-permute-start | bytes 373256 | tf_op jit(solution)/shard_map/ppermute | solution.py:59
  166.7 41.9 %copy-start.34 = (bf16[27,6,384]{2,1,0:T(8,128)(2,1)}, bf16[27,6,384]{2,1,0:T(8,128)(2,1)S(1)}, u32[]{:S(2)}) copy-start(bf16[27,6,384]{2,1,0:T(8,128)(2,1)S(1)} %collective-permute-done.30) | copy-start | bytes 373252
  166.7 6.0 %collective-permute-start.31 = (bf16[27,6,384]{2,1,0:T(8,128)(2,1)S(1)}, bf16[27,6,384]{2,1,0:T(8,128)(2,1)S(1)}, u32[]{:S(2)}, u32[]{:S(2)}) collective-permute-start(bf16[27,6,384]{2,1,0:T(8,128)(2,1)S(1)} %collective-permute-done.30), channel_id=1, source_target_pairs={{0,1},{1,2},{2,3},{3,4},{4,5},{5,6},{6,7},{7,8},{8,9},{9,10},{10,1... | collective-permute-start | bytes 373256 | tf_op jit(solution)/shard_map/ppermute | solution.py:59
  172.6 35.9 %copy-start.36 = (bf16[27,6,384]{2,1,0:T(8,128)(2,1)}, bf16[27,6,384]{2,1,0:T(8,128)(2,1)S(1)}, u32[]{:S(2)}) copy-start(bf16[27,6,384]{2,1,0:T(8,128)(2,1)S(1)} %collective-permute-done.31) | copy-start | bytes 373252
  172.6 6.0 %collective-permute-start.32 = (bf16[27,6,384]{2,1,0:T(8,128)(2,1)S(1)}, bf16[27,6,384]{2,1,0:T(8,128)(2,1)S(1)}, u32[]{:S(2)}, u32[]{:S(2)}) collective-permute-start(bf16[27,6,384]{2,1,0:T(8,128)(2,1)S(1)} %collective-permute-done.31), channel_id=1, source_target_pairs={{0,1},{1,2},{2,3},{3,4},{4,5},{5,6},{6,7},{7,8},{8,9},{9,10},{10,1... | collective-permute-start | bytes 373256 | tf_op jit(solution)/shard_map/ppermute | solution.py:59
  178.6 29.9 %copy-start.38 = (bf16[27,6,384]{2,1,0:T(8,128)(2,1)}, bf16[27,6,384]{2,1,0:T(8,128)(2,1)S(1)}, u32[]{:S(2)}) copy-start(bf16[27,6,384]{2,1,0:T(8,128)(2,1)S(1)} %collective-permute-done.32) | copy-start | bytes 373252
  178.6 6.0 %collective-permute-start.33 = (bf16[27,6,384]{2,1,0:T(8,128)(2,1)S(1)}, bf16[27,6,384]{2,1,0:T(8,128)(2,1)S(1)}, u32[]{:S(2)}, u32[]{:S(2)}) collective-permute-start(bf16[27,6,384]{2,1,0:T(8,128)(2,1)S(1)} %collective-permute-done.32), channel_id=1, source_target_pairs={{0,1},{1,2},{2,3},{3,4},{4,5},{5,6},{6,7},{7,8},{8,9},{9,10},{10,1... | collective-permute-start | bytes 373256 | tf_op jit(solution)/shard_map/ppermute | solution.py:59
  184.6 24.0 %copy-start.39 = (bf16[27,6,384]{2,1,0:T(8,128)(2,1)}, bf16[27,6,384]{2,1,0:T(8,128)(2,1)S(1)}, u32[]{:S(2)}) copy-start(bf16[27,6,384]{2,1,0:T(8,128)(2,1)S(1)} %collective-permute-done.33) | copy-start | bytes 373252
  184.6 6.0 %collective-permute-start.34 = (bf16[27,6,384]{2,1,0:T(8,128)(2,1)S(1)}, bf16[27,6,384]{2,1,0:T(8,128)(2,1)S(1)}, u32[]{:S(2)}, u32[]{:S(2)}) collective-permute-start(bf16[27,6,384]{2,1,0:T(8,128)(2,1)S(1)} %collective-permute-done.33), channel_id=1, source_target_pairs={{0,1},{1,2},{2,3},{3,4},{4,5},{5,6},{6,7},{7,8},{8,9},{9,10},{10,1... | collective-permute-start | bytes 373256 | tf_op jit(solution)/shard_map/ppermute | solution.py:59
  190.6 18.0 %copy-start.40 = (bf16[27,6,384]{2,1,0:T(8,128)(2,1)}, bf16[27,6,384]{2,1,0:T(8,128)(2,1)S(1)}, u32[]{:S(2)}) copy-start(bf16[27,6,384]{2,1,0:T(8,128)(2,1)S(1)} %collective-permute-done.34) | copy-start | bytes 373252
  190.6 6.0 %collective-permute-start.35 = (bf16[27,6,384]{2,1,0:T(8,128)(2,1)S(1)}, bf16[27,6,384]{2,1,0:T(8,128)(2,1)S(1)}, u32[]{:S(2)}, u32[]{:S(2)}) collective-permute-start(bf16[27,6,384]{2,1,0:T(8,128)(2,1)S(1)} %collective-permute-done.34), channel_id=1, source_target_pairs={{0,1},{1,2},{2,3},{3,4},{4,5},{5,6},{6,7},{7,8},{8,9},{9,10},{10,1... | collective-permute-start | bytes 373256 | tf_op jit(solution)/shard_map/ppermute | solution.py:59
  196.6 12.0 %copy-start.41 = (bf16[27,6,384]{2,1,0:T(8,128)(2,1)}, bf16[27,6,384]{2,1,0:T(8,128)(2,1)S(1)}, u32[]{:S(2)}) copy-start(bf16[27,6,384]{2,1,0:T(8,128)(2,1)S(1)} %collective-permute-done.35) | copy-start | bytes 373252
  196.6 6.0 %collective-permute-start.36 = (bf16[27,6,384]{2,1,0:T(8,128)(2,1)S(1)}, bf16[27,6,384]{2,1,0:T(8,128)(2,1)S(1)}, u32[]{:S(2)}, u32[]{:S(2)}) collective-permute-start(bf16[27,6,384]{2,1,0:T(8,128)(2,1)S(1)} %collective-permute-done.35), channel_id=1, source_target_pairs={{0,1},{1,2},{2,3},{3,4},{4,5},{5,6},{6,7},{7,8},{8,9},{9,10},{10,1... | collective-permute-start | bytes 373256 | tf_op jit(solution)/shard_map/ppermute | solution.py:59
  202.5 6.0 %collective-permute-start.37 = (bf16[27,6,384]{2,1,0:T(8,128)(2,1)S(1)}, bf16[27,6,384]{2,1,0:T(8,128)(2,1)S(1)}, u32[]{:S(2)}, u32[]{:S(2)}) collective-permute-start(bf16[27,6,384]{2,1,0:T(8,128)(2,1)S(1)} %collective-permute-done.36), channel_id=1, source_target_pairs={{0,1},{1,2},{2,3},{3,4},{4,5},{5,6},{6,7},{7,8},{8,9},{9,10},{10,1... | collective-permute-start | bytes 373256 | tf_op jit(solution)/shard_map/ppermute | solution.py:59
  208.5 6.1 %collective-permute-start.38 = (bf16[27,6,384]{2,1,0:T(8,128)(2,1)S(1)}, bf16[27,6,384]{2,1,0:T(8,128)(2,1)}, u32[]{:S(2)}, u32[]{:S(2)}) collective-permute-start(bf16[27,6,384]{2,1,0:T(8,128)(2,1)S(1)} %collective-permute-done.37), channel_id=1, source_target_pairs={{0,1},{1,2},{2,3},{3,4},{4,5},{5,6},{6,7},{7,8},{8,9},{9,10},{10,1... | collective-permute-start | bytes 373256 | tf_op jit(solution)/shard_map/ppermute | solution.py:59
  239.6 5.8 %collective-permute-start = (bf16[2,8,10,384]{3,2,1,0:T(8,128)(2,1)S(1)}, bf16[2,8,10,384]{3,2,1,0:T(8,128)(2,1)S(1)}, u32[]{:S(2)}, u32[]{:S(2)}) collective-permute-start(bf16[2,8,10,384]{3,2,1,0:T(8,128)(2,1)S(1)} %slice.512), channel_id=1, source_target_pairs={{0,64},{64,128},{128,192},{1,65},{65,129},{129,193},{2,66},{66,130... | collective-permute-start | bytes 368648 | tf_op jit(solution)/shard_map/ppermute | solution.py:10
  245.4 6.1 %collective-permute-start.1 = (bf16[6,1,10,384]{3,2,1,0:T(8,128)(2,1)S(1)}, bf16[6,1,10,384]{3,2,1,0:T(8,128)(2,1)S(1)}, u32[]{:S(2)}, u32[]{:S(2)}) collective-permute-start(bf16[6,1,10,384]{3,2,1,0:T(8,128)(2,1)S(1)} %get-tuple-element.72), channel_id=1, source_target_pairs={{0,16},{16,32},{32,48},{1,17},{17,33},{33,49},{2,18},{18,34},{34,5... | collective-permute-start | bytes 138248 | tf_op jit(solution)/shard_map/ppermute | solution.py:20
  248.6 5.1 %collective-permute-start.2 = (bf16[6,1,10,384]{3,2,1,0:T(8,128)(2,1)S(1)}, bf16[6,1,10,384]{3,2,1,0:T(8,128)(2,1)S(1)}, u32[]{:S(2)}, u32[]{:S(2)}) collective-permute-start(bf16[6,1,10,384]{3,2,1,0:T(8,128)(2,1)S(1)} %get-tuple-element.73), channel_id=1, source_target_pairs={{16,0},{32,16},{48,32},{17,1},{33,17},{49,33},{18,2},{34,18},{50,3... | collective-permute-start | bytes 138248 | tf_op jit(solution)/shard_map/ppermute | solution.py:21
  254.5 16.6 %collective-permute-start.19 = (bf16[6,10,1,384]{3,2,1,0:T(2,128)(2,1)}, bf16[6,10,1,384]{3,2,1,0:T(2,128)(2,1)S(1)}, u32[]{:S(2)}, u32[]{:S(2)}) collective-permute-start(bf16[6,10,1,384]{3,2,1,0:T(2,128)(2,1)} %get-tuple-element.49), channel_id=1, source_target_pairs={{1,0},{2,1},{3,2},{4,3},{5,4},{6,5},{7,6},{8,7},{9,8},{10,9},{11,1... | collective-permute-start | bytes 138248 | tf_op jit(solution)/shard_map/ppermute | solution.py:21
  263.7 7.4 %collective-permute-start.3 = (bf16[6,10,1,384]{3,2,1,0:T(2,128)(2,1)}, bf16[6,10,1,384]{3,2,1,0:T(2,128)(2,1)S(1)}, u32[]{:S(2)}, u32[]{:S(2)}) collective-permute-start(bf16[6,10,1,384]{3,2,1,0:T(2,128)(2,1)} %get-tuple-element.48), channel_id=1, source_target_pairs={{0,1},{1,2},{2,3},{3,4},{4,5},{5,6},{6,7},{7,8},{8,9},{9,10},{10,1... | collective-permute-start | bytes 138248 | tf_op jit(solution)/shard_map/ppermute | solution.py:20
  292.7 12.7 %copy-start.14 = (bf16[320,384]{1,0:T(8,128)(2,1)S(1)}, bf16[320,384]{1,0:T(8,128)(2,1)}, u32[]{:S(2)}) copy-start(bf16[320,384]{1,0:T(8,128)(2,1)} %reshape.204) | copy-start | bytes 737284
  294.2 10.9 %copy-start.24 = (bf16[320,384]{1,0:T(8,128)(2,1)S(1)}, bf16[320,384]{1,0:T(8,128)(2,1)}, u32[]{:S(2)}) copy-start(bf16[320,384]{1,0:T(8,128)(2,1)} %reshape.203) | copy-start | bytes 737284
  294.2 14.3 %copy-start.12 = (bf16[320,384]{1,0:T(8,128)(2,1)S(1)}, bf16[320,384]{1,0:T(8,128)(2,1)}, u32[]{:S(2)}) copy-start(bf16[320,384]{1,0:T(8,128)(2,1)} %reshape.207) | copy-start | bytes 737284
  295.8 13.0 %copy-start.20 = (bf16[320,384]{1,0:T(8,128)(2,1)S(1)}, bf16[320,384]{1,0:T(8,128)(2,1)}, u32[]{:S(2)}) copy-start(bf16[320,384]{1,0:T(8,128)(2,1)} %reshape.208) | copy-start | bytes 737284
  314.7 7.8 %collective-permute-start.20 = (bf16[2,8,10,384]{3,2,1,0:T(8,128)(2,1)S(1)}, bf16[2,8,10,384]{3,2,1,0:T(8,128)(2,1)S(1)}, u32[]{:S(2)}, u32[]{:S(2)}) collective-permute-start(bf16[2,8,10,384]{3,2,1,0:T(8,128)(2,1)S(1)} %slice.566), channel_id=1, source_target_pairs={{0,64},{64,128},{128,192},{1,65},{65,129},{129,193},{2,66},{66,130... | collective-permute-start | bytes 368648 | tf_op jit(solution)/shard_map/ppermute | solution.py:10
  322.6 6.3 %collective-permute-start.21 = (bf16[6,1,10,384]{3,2,1,0:T(8,128)(2,1)S(1)}, bf16[6,1,10,384]{3,2,1,0:T(8,128)(2,1)S(1)}, u32[]{:S(2)}, u32[]{:S(2)}) collective-permute-start(bf16[6,1,10,384]{3,2,1,0:T(8,128)(2,1)S(1)} %get-tuple-element.66), channel_id=1, source_target_pairs={{0,16},{16,32},{32,48},{1,17},{17,33},{33,49},{2,18},{18,34},{34,5... | collective-permute-start | bytes 138248 | tf_op jit(solution)/shard_map/ppermute | solution.py:20
  325.7 5.1 %collective-permute-start.22 = (bf16[6,1,10,384]{3,2,1,0:T(8,128)(2,1)S(1)}, bf16[6,1,10,384]{3,2,1,0:T(8,128)(2,1)S(1)}, u32[]{:S(2)}, u32[]{:S(2)}) collective-permute-start(bf16[6,1,10,384]{3,2,1,0:T(8,128)(2,1)S(1)} %get-tuple-element.67), channel_id=1, source_target_pairs={{16,0},{32,16},{48,32},{17,1},{33,17},{49,33},{18,2},{34,18},{50,3... | collective-permute-start | bytes 138248 | tf_op jit(solution)/shard_map/ppermute | solution.py:21
  328.9 12.0 %copy-start.27 = (bf16[6,1,10,384]{3,2,1,0:T(8,128)(2,1)}, bf16[6,1,10,384]{3,2,1,0:T(8,128)(2,1)S(1)}, u32[]{:S(2)}) copy-start(bf16[6,1,10,384]{3,2,1,0:T(8,128)(2,1)S(1)} %collective-permute-done.21) | copy-start | bytes 138244
  333.2 15.9 %collective-permute-start.23 = (bf16[6,10,1,384]{3,2,1,0:T(2,128)(2,1)}, bf16[6,10,1,384]{3,2,1,0:T(2,128)(2,1)}, u32[]{:S(2)}, u32[]{:S(2)}) collective-permute-start(bf16[6,10,1,384]{3,2,1,0:T(2,128)(2,1)} %get-tuple-element.26), channel_id=1, source_target_pairs={{0,1},{1,2},{2,3},{3,4},{4,5},{5,6},{6,7},{7,8},{8,9},{9,10},{10,1... | collective-permute-start | bytes 138248 | tf_op jit(solution)/shard_map/ppermute | solution.py:20
  335.2 14.0 %collective-permute-start.39 = (bf16[6,10,1,384]{3,2,1,0:T(2,128)(2,1)}, bf16[6,10,1,384]{3,2,1,0:T(2,128)(2,1)}, u32[]{:S(2)}, u32[]{:S(2)}) collective-permute-start(bf16[6,10,1,384]{3,2,1,0:T(2,128)(2,1)} %get-tuple-element.27), channel_id=1, source_target_pairs={{1,0},{2,1},{3,2},{4,3},{5,4},{6,5},{7,6},{8,7},{9,8},{10,9},{11,1... | collective-permute-start | bytes 138248 | tf_op jit(solution)/shard_map/ppermute | solution.py:21
  356.3 21.7 %copy-start.3 = (bf16[4,8,10,384]{3,2,1,0:T(8,128)(2,1)S(1)}, bf16[4,8,10,384]{3,2,1,0:T(8,128)(2,1)}, u32[]{:S(2)}) copy-start(bf16[4,8,10,384]{3,2,1,0:T(8,128)(2,1)} %get-tuple-element.7) | copy-start | bytes 737284
  356.3 21.9 %copy-start.2 = (bf16[4,8,10,384]{3,2,1,0:T(8,128)(2,1)S(1)}, bf16[4,8,10,384]{3,2,1,0:T(8,128)(2,1)}, u32[]{:S(2)}) copy-start(bf16[4,8,10,384]{3,2,1,0:T(8,128)(2,1)} %get-tuple-element.6) | copy-start | bytes 737284
  378.0 15.1 %copy-start.13 = (bf16[320,384]{1,0:T(8,128)(2,1)S(1)}, bf16[320,384]{1,0:T(8,128)(2,1)}, u32[]{:S(2)}) copy-start(bf16[320,384]{1,0:T(8,128)(2,1)} %reshape.235) | copy-start | bytes 737284
  378.2 16.1 %slice-start = ((s8[7962624]{0:T(1024)(128)(4,1)}), s8[4194304]{0:T(1024)(128)(4,1)S(1)}, s32[]{:S(2)}) async-start(s8[7962624]{0:T(1024)(128)(4,1)} %bitcast.217), calls=%async_computation.2 | async-start | bytes 8388608
  378.3 16.1 %copy-start.23 = (bf16[320,384]{1,0:T(8,128)(2,1)S(1)}, bf16[320,384]{1,0:T(8,128)(2,1)}, u32[]{:S(2)}) copy-start(bf16[320,384]{1,0:T(8,128)(2,1)} %reshape.236) | copy-start | bytes 737284
  381.3 13.5 %copy-start.22 = (bf16[320,384]{1,0:T(8,128)(2,1)S(1)}, bf16[320,384]{1,0:T(8,128)(2,1)}, u32[]{:S(2)}) copy-start(bf16[320,384]{1,0:T(8,128)(2,1)} %reshape.237) | copy-start | bytes 737284
  382.7 12.4 %copy-start.25 = (bf16[320,384]{1,0:T(8,128)(2,1)S(1)}, bf16[320,384]{1,0:T(8,128)(2,1)}, u32[]{:S(2)}) copy-start(bf16[320,384]{1,0:T(8,128)(2,1)} %reshape.238) | copy-start | bytes 737284
  384.2 11.3 %copy-start.21 = (bf16[320,384]{1,0:T(8,128)(2,1)S(1)}, bf16[320,384]{1,0:T(8,128)(2,1)}, u32[]{:S(2)}) copy-start(bf16[320,384]{1,0:T(8,128)(2,1)} %reshape.240) | copy-start | bytes 737284
  385.7 10.2 %copy-start.11 = (bf16[320,384]{1,0:T(8,128)(2,1)S(1)}, bf16[320,384]{1,0:T(8,128)(2,1)}, u32[]{:S(2)}) copy-start(bf16[320,384]{1,0:T(8,128)(2,1)} %reshape.241) | copy-start | bytes 737284
  (28 other events, 127.5 us)
Sparse Core Ops, SparseCore 0:
  123.9 87.0 all-gather.2
  239.2 87.0 all-gather.4
